TPU v7x, 32 devices: a whole 2x2x4 slice. The times are simulated.
32 devices in a mesh: prow: 8 (over z, y), pcol: 4 (over x, core).
Axes of the slice: x: 2, y: 2, z: 4, core: 2. Of those that a mesh axis runs over, the one named last changes fastest.
Arguments:
- panel_rows: float32 [2, 1024, 12288], P(None, None, ('prow', 'pcol')), may hold values from -0.109375 to 0.109375
- solved: float32 [12288, 1024], P(('prow', 'pcol')), may hold values from -6 to 6
- right_side: float32 [2, 1024, 1024], P(None, 'prow', 'pcol'), may hold values from -6 to 6
- coupling: float32 [1024, 1024], P(None, 'prow'), may hold values from -0.1875 to 0.1875
- inverses: float32 [2, 1024, 1024], P(None, 'prow'), may hold values from -2 to 2, as said below
Outputs:
- panels: float32 [2, 1024, 1024], P(None, 'prow', 'pcol')
Inputs may be any that keep to these rules, and one draw needn't show every extreme that they name: `inverses`: each tile is zero above its diagonal, and its diagonal entries are positive.
All inputs are finite; a program needn't handle non-finite values.
Results may differ from a plain program's by a relative error of at most 0.000088.
Values sent between devices are 32-bit elements; how exact they have to be, the bound alone decides.
A program may use at most 64 MiB of HBM per device.

v0:
```python
import jax
import jax.numpy as jnp
from jax import lax
from jax.sharding import PartitionSpec as P


def combine_old(partial_value):
    by_samples = lax.psum_scatter(partial_value, "pcol", scatter_dimension=2, tiled=True)
    return lax.psum_scatter(by_samples, "prow", scatter_dimension=1, tiled=True)


def apply_inverse(inverse_rows, residue):
    highest = lax.Precision.HIGHEST
    return jnp.dot(
        inverse_rows,
        lax.all_gather(residue, "prow", axis=0, tiled=True),
        precision=highest,
        preferred_element_type=jnp.float32,
    )


def body(panel_rows, solved, right_side, coupling, inverses):
    highest = lax.Precision.HIGHEST
    tile_rows = panel_rows.shape[1]
    solved_rows = panel_rows.shape[2]
    flat_rows = panel_rows.reshape(2 * tile_rows, solved_rows)
    partial_value = jnp.dot(
        flat_rows, solved, precision=highest, preferred_element_type=jnp.float32
    )
    partial_value = partial_value.reshape(2, tile_rows, solved.shape[1])
    reduced = combine_old(partial_value)
    first_panel = apply_inverse(inverses[0], right_side[0] - reduced[0])
    coupling_term = jnp.dot(
        coupling, first_panel, precision=highest, preferred_element_type=jnp.float32
    )
    coupling_part = lax.psum_scatter(coupling_term, "prow", scatter_dimension=0, tiled=True)
    second_rest = right_side[1] - reduced[1] - coupling_part
    second_panel = apply_inverse(inverses[1], second_rest)
    return jnp.stack([first_panel, second_panel])


def solution(mesh):
    return jax.shard_map(
        body,
        mesh=mesh,
        in_specs=(
            P(None, None, ("prow", "pcol")),
            P(("prow", "pcol"), None),
            P(None, "prow", "pcol"),
            P(None, "prow"),
            P(None, "prow", None),
        ),
        out_specs=P(None, "prow", "pcol"),
        check_vma=False,
    )
```

profile of v0, /device:TPU:24, one launch (start us, length us, event | category | flops | bytes accessed | tf_op | source)
XLA Modules:
  0.0 330.3 jit_solution(222700605038099147)
XLA Ops:
  6.5 0.0 copy-start
  6.5 0.0 reduce-scatter.4.cloned.1.call-start
  6.5 1.9 copy-done
  8.4 16.7 %fusion = f32[2,1024,1024]{2,1,0:T(8,128)} fusion(f32[2,1024,384]{2,1,0:T(8,128)S(1)} %copy-done, f32[384,1024]{1,0:T(8,128)} %param.6), kind=kOutput, calls=%fused_computation | convolution fusion | flops 9663676416 | bytes 13107200 | tf_op jit(solution)/shard_map/dot_general | solution.py:27
  25.1 0.0 copy-start.1
  25.1 0.0 reduce-scatter.4.cloned.1.call-update
  25.2 0.0 reduce-scatter.6.cloned.1.call-start
  25.2 72.8 %reduce-scatter.4.cloned.1.call-done = f32[2,1024,256]{2,1,0:T(8,128)} async-done(((f32[2,1024,1024]{2,1,0:T(8,128)}), f32[2,1024,256]{2,1,0:T(8,128)}) %reduce-scatter.4.cloned.1.call-update) | async-done | bytes 2097168 | tf_op jit(solution)/shard_map/reduce_scatter | solution.py:8
  98.0 0.0 reduce-scatter.6.cloned.1.call-update
  98.1 0.0 all-gather.6.cloned.1.call-start
  98.1 70.4 %reduce-scatter.6.cloned.1.call-done = f32[2,128,256]{2,1,0:T(8,128)} async-done(((f32[2,1024,256]{2,1,0:T(8,128)}), f32[2,128,256]{2,1,0:T(8,128)}) %reduce-scatter.6.cloned.1.call-update) | async-done | bytes 262160 | tf_op jit(solution)/shard_map/reduce_scatter | solution.py:9
  168.5 0.0 copy-done.1
  168.5 1.6 slice_subtract_fusion.1
  170.1 0.0 all-gather.6.cloned.1.call-update
  170.1 0.0 reduce-scatter.8.cloned.1.call-start
  170.2 39.9 %all-gather.6.cloned.1.call-done = f32[1,1024,256]{2,1,0:T(8,128)} async-done(((f32[1,128,256]{2,1,0:T(8,128)}), f32[1,1024,256]{2,1,0:T(8,128)}) %all-gather.6.cloned.1.call-update) | async-done | bytes 1048592 | tf_op jit(solution)/shard_map/all_gather | solution.py:16
  210.1 3.2 fusion.2
  213.3 3.0 convolution_bitcast_fusion
  216.3 0.0 reduce-scatter.8.cloned.1.call-update
  216.3 0.0 all-gather.4.cloned.1.call-start
  216.3 62.2 %reduce-scatter.8.cloned.1.call-done = f32[128,256]{1,0:T(8,128)} async-done(((f32[1024,256]{1,0:T(8,128)}), f32[128,256]{1,0:T(8,128)}) %reduce-scatter.8.cloned.1.call-update) | async-done | bytes 131088 | tf_op jit(solution)/shard_map/reduce_scatter | solution.py:36
  278.6 1.6 fusion.9
  280.2 0.0 all-gather.4.cloned.1.call-update
  280.2 39.5 %all-gather.4.cloned.1.call-done = f32[1024,256]{1,0:T(8,128)} async-done(((f32[128,256]{1,0:T(8,128)}), f32[1024,256]{1,0:T(8,128)}) %all-gather.4.cloned.1.call-update) | async-done | bytes 1048592 | tf_op jit(solution)/shard_map/all_gather | solution.py:16
  319.7 3.2 convolution_bitcast_fusion.1
  322.9 0.8 copy.6
  (1 shorter events, 0.0 us)
Async XLA Ops:
  6.5 1.9 copy-start
  6.5 91.5 %reduce-scatter.4.cloned.1.call-start = ((), (), s32[]{:S(2)}) async-start(), calls=%async_computation.3 | async-start | bytes 10485760 | tf_op jit(solution)/shard_map/reduce_scatter | solution.py:8
  25.1 143.4 %copy-start.1 = (f32[2,128,256]{2,1,0:T(8,128)S(1)}, f32[2,128,256]{2,1,0:T(8,128)}, u32[]{:S(2)}) copy-start(f32[2,128,256]{2,1,0:T(8,128)} %param.7) | copy-start | bytes 786436
  25.2 143.4 %reduce-scatter.6.cloned.1.call-start = ((), (), s32[]{:S(2)}) async-start(), calls=%async_computation.4 | async-start | bytes 2359296 | tf_op jit(solution)/shard_map/reduce_scatter | solution.py:9
  98.1 112.0 %all-gather.6.cloned.1.call-start = ((), (), s32[]{:S(2)}) async-start(), calls=%async_computation.7 | async-start | bytes 1179648 | tf_op jit(solution)/shard_map/all_gather | solution.py:16
  170.1 108.4 %reduce-scatter.8.cloned.1.call-start = ((), (), s32[]{:S(2)}) async-start(), calls=%async_computation.5 | async-start | bytes 1179648 | tf_op jit(solution)/shard_map/reduce_scatter | solution.py:36
  216.3 103.4 %all-gather.4.cloned.1.call-start = ((), (), s32[]{:S(2)}) async-start(), calls=%async_computation.6 | async-start | bytes 1179648 | tf_op jit(solution)/shard_map/all_gather | solution.py:16
Sparse Core Ops, SparseCore 0:
  25.3 72.6 reduce-scatter.3
  102.0 66.5 reduce-scatter.5
  170.9 39.1 all-gather.5
  216.4 62.1 reduce-scatter.7
  280.5 39.1 all-gather.3
where the time goes:
time: 334 us; the launch traced here: 330 us
  waiting for transfers between devices  285 us (85%)
  matrix products  26 us (8%)
  between operations  13.2 us (4%)
    all_gather x2, waiting for transfers between devices, apply_inverse(): lax.all_gather(residue, 'prow', axis=0, tiled=True)  79.4 us
    reduce_scatter x1, waiting for transfers between devices, combine_old(): lax.psum_scatter(partial_value, 'pcol', scatter_dimension=2, tiled=True)  72.8 us
    reduce_scatter x1, waiting for transfers between devices, combine_old(): return lax.psum_scatter(by_samples, 'prow', scatter_dimension=1, tiled=True)  70.4 us
    reduce_scatter x1, waiting for transfers between devices, body(): lax.psum_scatter(coupling_term, 'prow', scatter_dimension=0, tiled=True)  62.2 us
    dot_general x1, matrix products, body(): jnp.dot(flat_rows, solved, precision=highest, preferred_element_type=jnp....  16.7 us
  transfers between devices with their start and end apart: 5, of which 5 were waited for; matrix products, arithmetic and copies ran while one was open for 0% of the time, Pallas kernels for 0%

commit v1 on v0

v1 whole, which is shorter than its diff:
```python
import functools

import jax
import jax.numpy as jnp
from jax import lax
from jax.experimental import pallas as pl
from jax.experimental.pallas import tpu as pltpu
from jax.sharding import PartitionSpec as P

MESH = pl.DeviceIdType.MESH
F32 = jnp.float32
BF16 = jnp.bfloat16


def split(value):
    high = value.astype(BF16)
    return high, (value - high.astype(F32)).astype(BF16)


def product(left_high, left_low, right_high, right_low):
    dot = functools.partial(jnp.dot, preferred_element_type=F32)
    small = dot(left_low, right_high) + dot(left_high, right_low)
    return small + dot(left_high, right_high)


def kernel(
    sizes, panel, solved, right_side, coupling, inverses, out,
    left0, left1, right, inv_high, inv_low,
    send0, recv0, own0, send1, recv1, own1,
    x_first, y_first, y_second, x_second, z_last, x_one,
    gathered, coupled, y_coupled, z_coupled,
    core0_s, core0_r, core1_s, core1_r, xf_s, xf_r, yf_s, yf_r, ys_s, ys_r,
    xs_s, xs_r, zl_s, zl_r, xo_s, xo_r, gz_s, gz_r, gy_s, gy_r, yc_s, yc_r, zc_s, zc_r,
):
    A, B, X, K, tr, hr, cw = sizes
    row, col = lax.axis_index("prow"), lax.axis_index("pcol")
    a, b = row // B, row % B
    x, c = col // 2, col % 2
    other_b, other_c = 1 - b, 1 - c

    def at(a_, b_, x_, c_):
        return (a_ * B + b_, x_ * 2 + c_)

    core_peer = at(a, b, x, other_c)
    y_peer = at(a, other_b, x, c)

    def x_peer(d):
        return at(a, b, lax.rem(x + d, X), c)

    def z_peer(d):
        return at(lax.rem(a + d, A), b, x, c)

    peers = [core_peer, y_peer]
    peers += [x_peer(d) for d in range(1, X)] + [z_peer(d) for d in range(1, A)]
    barrier = pltpu.get_barrier_semaphore()
    for peer in peers:
        pl.semaphore_signal(barrier, inc=1, device_id=peer, device_id_type=MESH)

    def copy(src, dst, s, r, peer):
        return pltpu.make_async_remote_copy(
            src_ref=src, dst_ref=dst, send_sem=s, recv_sem=r,
            device_id=peer, device_id_type=MESH,
        )

    def split_right(q):
        high, low = split(solved[:, q * cw:(q + 1) * cw])
        right[q, 0:K] = high
        right[q, K:2 * K] = low
        right[q, 2 * K:] = high

    def split_left(dst, value):
        high, low = split(value)
        dst[:, 0:K] = high
        dst[:, K:2 * K] = high
        dst[:, 2 * K:] = low

    for q in range(2 * X):
        split_right(q)
    for h in range(2):
        for b_ in range(B):
            split_left(left0.at[h, b_], panel[0, :, b_, h].reshape(A * hr, K))

    pl.semaphore_wait(barrier, len(peers))

    core0, core1 = {}, {}
    for h in range(2):
        lhs = left0.at[h]

        @pl.loop(0, X)
        def _(x_):
            value = jnp.dot(lhs[...].reshape(B * A * hr, 3 * K), right[x_ * 2 + other_c], preferred_element_type=F32)
            send0[h, x_] = value.reshape(B, A, hr, cw)
            copy(send0.at[h, x_], recv0.at[h, x_], core0_s.at[h, x_], core0_r.at[h, x_], core_peer).start()

    flying = []
    for h in range(2):
        lhs = left0.at[h]

        @pl.loop(0, X)
        def _(x_):
            value = jnp.dot(lhs[...].reshape(B * A * hr, 3 * K), right[x_ * 2 + c], preferred_element_type=F32)
            copy(send0.at[h, x_], recv0.at[h, x_], core0_s.at[h, x_], core0_r.at[h, x_], core_peer).wait()
            own0[h, x_] = value.reshape(B, A, hr, cw) + recv0[h, x_]

        if h == 0:
            first = [copy(own0.at[0, lax.rem(x + d, X)], x_first.at[d - 1], xf_s.at[d - 1], xf_r.at[d - 1], x_peer(d)) for d in range(1, X)]
            for each in first:
                each.start()
        else:
            first_v = copy(own0.at[1, :, other_b], y_first, yf_s, yf_r, y_peer)
            first_v.start()

    for b_ in range(B):
        split_left(left1.at[b_], panel[1, :, b_].reshape(A * tr, K))
    for b_ in range(B):
        lhs = left1.at[b_]

        @pl.loop(0, X)
        def _(x_):
            value = jnp.dot(lhs[...], right[x_ * 2 + other_c], preferred_element_type=F32)
            send1[x_, b_] = value.reshape(A, tr, cw)
            copy(send1.at[x_, b_], recv1.at[x_, b_], core1_s.at[x_, b_], core1_r.at[x_, b_], core_peer).start()

    for b_ in range(B):
        lhs = left1.at[b_]

        @pl.loop(0, X)
        def _(x_):
            value = jnp.dot(lhs[...], right[x_ * 2 + c], preferred_element_type=F32)
            copy(send1.at[x_, b_], recv1.at[x_, b_], core1_s.at[x_, b_], core1_r.at[x_, b_], core_peer).wait()
            own1[x_, b_] = value.reshape(A, tr, cw) + recv1[x_, b_]

    for p in range(2):
        high, low = split(inverses[p])
        inv_high[p] = high
        inv_low[p] = low

    for each in first:
        each.wait()
    total = own0[0, x]
    for d in range(1, X):
        total = total + x_first[d - 1]
    own0[0, x] = total
    second = copy(own0.at[0, x, other_b], y_second, ys_s, ys_r, y_peer)
    second.start()
    first_v.wait()
    for x_ in range(X):
        own0[1, x_, b] = own0[1, x_, b] + y_first[x_]
    second_v = [copy(own0.at[1, lax.rem(x + d, X), b], x_second.at[d - 1], xs_s.at[d - 1], xs_r.at[d - 1], x_peer(d)) for d in range(1, X)]
    for each in second_v:
        each.start()
    one = [copy(own1.at[lax.rem(x + d, X)], x_one.at[d - 1], xo_s.at[d - 1], xo_r.at[d - 1], x_peer(d)) for d in range(1, X)]
    for each in one:
        each.start()

    last = []
    second.wait()
    own0[0, x, b] = own0[0, x, b] + y_second[...]
    for h in range(2):
        if h == 1:
            for each in second_v:
                each.wait()
            total = own0[1, x, b]
            for d in range(1, X):
                total = total + x_second[d - 1]
            own0[1, x, b] = total
        for d in range(1, A):
            each = copy(own0.at[h, x, b, lax.rem(a + d, A)], z_last.at[h, d - 1], zl_s.at[h, d - 1], zl_r.at[h, d - 1], z_peer(d))
            each.start()
            last.append(each)
    for each in last:
        each.wait()
    for h in range(2):
        total = own0[h, x, b, a]
        for d in range(1, A):
            total = total + z_last[h, d - 1]
        gathered[0, a, b, h * hr:(h + 1) * hr] = right_side[0, h * hr:(h + 1) * hr] - total

    def gather(p):
        shard = gathered.at[p, a, b]
        along_z = [copy(shard, shard, gz_s.at[p, d], gz_r.at[p, d], z_peer(d)) for d in range(1, A)]
        for each in along_z:
            each.start()
        along_y = [copy(shard, shard, gy_s.at[p, 0], gy_r.at[p, 0], y_peer)]
        along_y[0].start()
        for d in range(1, A):
            along_z[d - 1].wait()
            got = gathered.at[p, lax.rem(a + A - d, A), b]
            along_y.append(copy(got, got, gy_s.at[p, d], gy_r.at[p, d], y_peer))
            along_y[-1].start()
        for each in along_y:
            each.wait()
        high, low = split(gathered[p].reshape(A * B * tr, cw))
        return product(inv_high[p], inv_low[p], high, low)

    first_panel = gather(0)
    out[0] = first_panel
    panel_high, panel_low = split(first_panel)

    for each in one:
        each.wait()
    along_y, along_z = [], []

    def term(b_):
        high, low = split(coupling[:, b_].reshape(A * tr, tr))
        value = product(high, low, panel_high, panel_low).reshape(A, tr, cw) + own1[x, b_]
        for d in range(1, X):
            value = value + x_one[d - 1, b_]
        return value

    coupled[0] = term(other_b)
    for d in list(range(1, A)) + [0]:
        a_ = lax.rem(a + d, A)
        each = copy(coupled.at[0, a_], y_coupled.at[a_], yc_s.at[d], yc_r.at[d], y_peer)
        each.start()
        along_y.append(each)
    coupled[1] = term(b)
    for d in range(1, A):
        a_ = lax.rem(a + d, A)
        along_y[d - 1].wait()
        coupled[1, a_] = coupled[1, a_] + y_coupled[a_]
        each = copy(coupled.at[1, a_], z_coupled.at[d - 1], zc_s.at[d - 1], zc_r.at[d - 1], z_peer(d))
        each.start()
        along_z.append(each)
    along_y[-1].wait()
    total = coupled[1, a] + y_coupled[a]
    for d in range(1, A):
        along_z[d - 1].wait()
        total = total + z_coupled[d - 1]
    gathered[1, a, b] = right_side[1] - total
    out[1] = gather(1)


def body(R, C, panel_rows, solved, right_side, coupling, inverses):
    B = 2
    A, X = R // B, C // 2
    K = panel_rows.shape[2]
    tr, cw = right_side.shape[1:]
    hr = tr // 2
    vmem, dma = pltpu.VMEM, pltpu.SemaphoreType.DMA
    steps = [(2, X), (X, B), (max(X - 1, 1),), (), (), (max(X - 1, 1),), (2, A - 1), (X - 1,), (2, A), (2, A), (A,), (A - 1,)]
    sems = []
    for shape in steps:
        sems += [dma(shape) if shape else dma, dma(shape) if shape else dma]
    return pl.pallas_call(
        functools.partial(kernel, (A, B, X, K, tr, hr, cw)),
        out_shape=jax.ShapeDtypeStruct((2, tr, cw), F32),
        in_specs=[pl.BlockSpec(memory_space=pltpu.VMEM)] * 5,
        out_specs=pl.BlockSpec(memory_space=pltpu.VMEM),
        scratch_shapes=[
            vmem((2, B, A * hr, 3 * K), BF16),
            vmem((B, A * tr, 3 * K), BF16),
            vmem((C, 3 * K, cw), BF16),
            vmem((2, tr, R * tr), BF16),
            vmem((2, tr, R * tr), BF16),
            vmem((2, X, B, A, hr, cw), F32),
            vmem((2, X, B, A, hr, cw), F32),
            vmem((2, X, B, A, hr, cw), F32),
            vmem((X, B, A, tr, cw), F32),
            vmem((X, B, A, tr, cw), F32),
            vmem((X, B, A, tr, cw), F32),
            vmem((X - 1, B, A, hr, cw), F32),
            vmem((X, A, hr, cw), F32),
            vmem((A, hr, cw), F32),
            vmem((X - 1, A, hr, cw), F32),
            vmem((2, A - 1, hr, cw), F32),
            vmem((X - 1, B, A, tr, cw), F32),
            vmem((2, A, B, tr, cw), F32),
            vmem((2, A, tr, cw), F32),
            vmem((A, tr, cw), F32),
            vmem((A - 1, tr, cw), F32),
        ] + sems,
        compiler_params=pltpu.CompilerParams(
            collective_id=0, has_side_effects=True, vmem_limit_bytes=56 << 20
        ),
    )(
        panel_rows.reshape(2, A, B, 2, hr, K),
        solved,
        right_side,
        coupling.reshape(A, B, tr, tr),
        inverses,
    )


def solution(mesh):
    return jax.shard_map(
        functools.partial(body, mesh.shape["prow"], mesh.shape["pcol"]),
        mesh=mesh,
        in_specs=(
            P(None, None, ("prow", "pcol")),
            P(("prow", "pcol"), None),
            P(None, "prow", "pcol"),
            P(None, "prow"),
            P(None, "prow", None),
        ),
        out_specs=P(None, "prow", "pcol"),
        check_vma=False,
    )
```

time: 334 us -> 100 us (0.30)
  waiting for transfers between devices: 285 us -> 0 us
  Pallas kernels: 0 us -> 97.5 us
  matrix products: 26 us -> 0 us
  between operations: 13.2 us -> 0.01 us
    reduce_scatter x3 -> x0, waiting for transfers between devices: 205 us -> none  [the longest x1 72.8 us: combine_old(): lax.psum_scatter(partial_value, 'pcol', scatter_dimension=2, tiled=True)]
    pallas_call x0 -> x1, Pallas kernels: none -> 97.5 us  [body(): pl.pallas_call(functools.partial(kernel, (A, B, X, K, tr, hr, cw)), out_s...]
    all_gather x2 -> x0, waiting for transfers between devices: 79.4 us -> none  [apply_inverse(): lax.all_gather(residue, 'prow', axis=0, tiled=True)]
    dot_general x4 -> x0, matrix products: 26 us -> none  [the longest x1 16.7 us: body(): jnp.dot(flat_rows, solved, precision=highest, preferred_element_type=jnp....]
  transfers between devices with their start and end apart: 5 -> 0, of which waited for: 5 -> 0; matrix products, arithmetic and copies ran while one was open for 0% -> 0% of each run, Pallas kernels for 0% -> 0%
where the time goes in v1:
time: 100 us; the launch traced here: 99.1 us
  Pallas kernels  97.5 us (98%)
  local copies, waits for them, and re-layouts  1.67 us (2%)
    pallas_call x1, Pallas kernels, body(): pl.pallas_call(functools.partial(kernel, (A, B, X, K, tr, hr, cw)), out_s...  97.5 us

profile of v1, /device:TPU:24, one launch (start us, length us, event | category | flops | bytes accessed | tf_op | source)
XLA Modules:
  0.0 99.1 jit_solution(3234233357613731468)
XLA Ops:
  0.0 97.5 %shard_map.55 = f32[2,128,256]{2,1,0:T(8,128)} custom-call(f32[2,4,2,2,64,384]{5,4,3,2,1,0:T(8,128)} %bitcast.2, f32[384,1024]{1,0:T(8,128)} %solved.1, f32[2,128,256]{2,1,0:T(8,128)} %right_side.1, f32[4,2,128,128]{3,2,1,0:T(8,128)} %bitcast.3, f32[2,128,1024]{2,1,0:T(8,128)} %inverses.1), custom_call_target="tpu_custom_call" | custom-call | tf_op jit(solution)/shard_map/pallas_call | solution.py:245
  97.5 1.7 %copy.7 = f32[2,128,256]{2,1,0:T(8,128)} copy(f32[2,128,256]{2,1,0:T(8,128)} %shard_map.55) | data formatting | bytes 524288

commit v2 on v0

v2 whole, which is shorter than its diff:
```python
import functools

import jax
import jax.numpy as jnp
from jax import lax
from jax.experimental import pallas as pl
from jax.experimental.pallas import tpu as pltpu
from jax.sharding import PartitionSpec as P

MESH = pl.DeviceIdType.MESH
F32 = jnp.float32
BF16 = jnp.bfloat16


def split(value):
    high = value.astype(BF16)
    return high, (value - high.astype(F32)).astype(BF16)


def product(left_high, left_low, right_high, right_low):
    dot = functools.partial(jnp.dot, preferred_element_type=F32)
    small = dot(left_low, right_high) + dot(left_high, right_low)
    return small + dot(left_high, right_high)


def kernel(
    sizes, panel, solved, right_side, coupling, inverses, out,
    left, right, sent, received, own, x_u, y_v, y_u, x_v, z_last,
    side_cut, side, inv_got, inv_high, inv_low, coup_got, coup_high, coup_low,
    gathered, coupled, z_coupled, block_high, block_low, mine, theirs,
    side_s, side_r, iy_s, iy_r, ic_s, ic_r, cy_s, cy_r, cc_s, cc_r,
    core_s, core_r, xu_s, xu_r, yv_s, yv_r, yu_s, yu_r, xv_s, xv_r,
    zl_s, zl_r, g0_s, g0_r, zc_s, zc_r, g1_s, g1_r, end_s, end_r,
):
    A, B, X, K, tr, qr, cw = sizes
    half = cw // 2
    block = B * tr
    row, col = lax.axis_index("prow"), lax.axis_index("pcol")
    a, b = row // B, row % B
    x, c = col // 2, col % 2
    other_b, other_c = 1 - b, 1 - c

    def at(a_, b_, x_, c_):
        return (a_ * B + b_, x_ * 2 + c_)

    core_peer = at(a, b, x, other_c)
    y_peer = at(a, other_b, x, c)

    def x_peer(d):
        return at(a, b, lax.rem(x + d, X), c)

    def z_peer(d):
        return at(lax.rem(a + d, A), b, x, c)

    peers = [core_peer, y_peer]
    peers += [x_peer(d) for d in range(1, X)] + [z_peer(d) for d in range(1, A)]
    barrier = pltpu.get_barrier_semaphore()
    for peer in peers:
        pl.semaphore_signal(barrier, inc=1, device_id=peer, device_id_type=MESH)

    def copy(src, dst, s, r, peer):
        return pltpu.make_async_remote_copy(
            src_ref=src, dst_ref=dst, send_sem=s, recv_sem=r,
            device_id=peer, device_id_type=MESH,
        )

    for b_ in range(B):
        side_cut[b_] = right_side[:, :, b_ * half:(b_ + 1) * half]
    side[:, b] = side_cut[b]

    def split_right(q):
        high, low = split(solved[:, q * cw:(q + 1) * cw])
        right[q, 0:K] = high
        right[q, K:2 * K] = low
        right[q, 2 * K:] = high

    def split_left(t):
        for v in range(2):
            high, low = split(panel[t // 2, :, t % 2, v].reshape(A * qr, K))
            left[t, v, :, 0:K] = high
            left[t, v, :, K:2 * K] = high
            left[t, v, :, 2 * K:] = low

    pl.semaphore_wait(barrier, len(peers))

    def inverse_y(p):
        return copy(inverses.at[p, c], inv_got.at[p, c], iy_s.at[p], iy_r.at[p], y_peer)

    def inverse_core(p):
        return copy(inv_got.at[p, c], inv_got.at[p, c], ic_s.at[p], ic_r.at[p], core_peer)

    coupling_y = copy(coupling.at[c], coup_got.at[c], cy_s, cy_r, y_peer)
    coupling_core = copy(coup_got.at[c], coup_got.at[c], cc_s, cc_r, core_peer)
    side_y = copy(side_cut.at[other_b], side.at[:, b], side_s, side_r, y_peer)
    inverse_y(0).start()
    side_y.start()

    for q in range(2 * X):
        split_right(q)

    def multiply(t, q):
        lhs = left[t].reshape(2 * A * qr, 3 * K)
        return jnp.dot(lhs, right[q], preferred_element_type=F32).reshape(2, A, qr, cw)

    def core(t, x_):
        return copy(sent.at[t, x_], received.at[t, x_], core_s.at[t, x_], core_r.at[t, x_], core_peer)

    def compute(t):
        split_left(t)

        @pl.loop(0, X)
        def _(x_):
            value = multiply(t, x_ * 2 + other_c)
            for b_ in range(B):
                sent[t, x_, :, b_] = value[..., b_ * half:(b_ + 1) * half]
            core(t, x_).start()

        @pl.loop(0, X)
        def _(x_):
            value = multiply(t, x_ * 2 + c)
            core(t, x_).wait()
            for b_ in range(B):
                own[t, x_, :, b_] = value[..., b_ * half:(b_ + 1) * half] + received[t, x_, :, b_]

    def first_u(t):
        return [copy(own.at[t, lax.rem(x + d, X), 0], x_u.at[t, d - 1], xu_s.at[t, d - 1], xu_r.at[t, d - 1], x_peer(d)) for d in range(1, X)]

    def first_v(t):
        return [copy(own.at[t, :, 1, other_b], y_v.at[t], yv_s.at[t], yv_r.at[t], y_peer)]

    def second_u(t):
        return [copy(own.at[t, x, 0, other_b], y_u.at[t], yu_s.at[t], yu_r.at[t], y_peer)]

    def second_v(t):
        return [copy(own.at[t, lax.rem(x + d, X), 1, b], x_v.at[t, d - 1], xv_s.at[t, d - 1], xv_r.at[t, d - 1], x_peer(d)) for d in range(1, X)]

    def start(copies):
        for each in copies:
            each.start()

    def wait(copies):
        for each in copies:
            each.wait()

    def start_first(t):
        start(first_u(t))
        start(first_v(t))

    def turn(t):
        wait(first_u(t))
        for b_ in range(B):
            total = own[t, x, 0, b_]
            for d in range(1, X):
                total = total + x_u[t, d - 1, b_]
            own[t, x, 0, b_] = total
        start(second_u(t))
        wait(first_v(t))
        for x_ in range(X):
            own[t, x_, 1, b] = own[t, x_, 1, b] + y_v[t, x_]
        start(second_v(t))

    def finish(t):
        wait(second_u(t))
        own[t, x, 0, b] = own[t, x, 0, b] + y_u[t]
        wait(second_v(t))
        total = own[t, x, 1, b]
        for d in range(1, X):
            total = total + x_v[t, d - 1]
        own[t, x, 1, b] = total

    def along_z(t):
        return [copy(own.at[t, x, :, b, lax.rem(a + d, A)], z_last.at[t, d - 1], zl_s.at[t, d - 1], zl_r.at[t, d - 1], z_peer(d)) for d in range(1, A)]

    def gather_first(g):
        shard = gathered.at[0, a, g]
        return [copy(shard, shard, g0_s.at[g, d - 1], g0_r.at[g, d - 1], z_peer(d)) for d in range(1, A)]

    def rest(g):
        wait(along_z(g))
        for v in range(2):
            total = own[g, x, v, b, a]
            for d in range(1, A):
                total = total + z_last[g, d - 1, v]
            at_row = (g * 2 + v) * qr
            gathered[0, a, g, v * qr:(v + 1) * qr] = side[0, at_row // tr, at_row % tr:at_row % tr + qr] - total
        start(gather_first(g))

    def hold_inverse(p, b_, value):
        for a_ in range(A):
            high, low = split(value[:, a_ * block:(a_ + 1) * block])
            inv_high[p, a_, b_] = high
            inv_low[p, a_, b_] = low

    def got_inverse(p):
        inverse_core(p).wait()
        hold_inverse(p, other_b, inv_got[p].reshape(tr, A * block))

    def times_inverse(p, a_):
        high, low = split(gathered[p, a_].reshape(block, half))
        shape = (block, block)
        return product(inv_high[p, a_].reshape(shape), inv_low[p, a_].reshape(shape), high, low)

    compute(0)
    start_first(0)
    compute(1)
    turn(0)
    start_first(1)
    inverse_y(0).wait()
    inverse_core(0).start()
    compute(2)
    finish(0)
    start(along_z(0))
    turn(1)
    start_first(2)
    coupling_y.start()
    compute(3)
    finish(1)
    start(along_z(1))
    turn(2)
    start_first(3)
    side_y.wait()
    rest(0)
    hold_inverse(0, b, inverses[0].reshape(tr, A * block))
    got_inverse(0)
    rest(1)
    high, low = split(coupling[...].reshape(A, block, tr))
    coup_high[:, :, 0:tr] = high
    coup_low[:, :, 0:tr] = low
    coupling_y.wait()
    coupling_core.start()
    finish(2)
    turn(3)
    inverse_y(1).start()
    coupling_core.wait()
    high, low = split(coup_got[...].reshape(A, block, tr))
    coup_high[:, :, tr:] = high
    coup_low[:, :, tr:] = low
    hold_inverse(1, b, inverses[1].reshape(tr, A * block))

    first_panel = times_inverse(0, a)
    for d in range(1, A):
        for g in range(2):
            gather_first(g)[d - 1].wait()
        first_panel = first_panel + times_inverse(0, lax.rem(a + A - d, A))

    def finalize(p, value):
        mine[p] = value.reshape(B, tr, half)
        return copy(mine.at[p, other_b], theirs.at[p], end_s.at[p], end_r.at[p], y_peer)

    def result(p):
        ours, got = mine[p, b], theirs[p]
        out[p, :, 0:half] = jnp.where(b == 0, ours, got)
        out[p, :, half:] = jnp.where(b == 0, got, ours)

    end_first = finalize(0, first_panel)
    end_first.start()
    for each, ref in zip(split(first_panel.reshape(B, tr, half)), (block_high, block_low)):
        ref[...] = each
    finish(3)

    def ordered(ref):
        return jnp.concatenate([ref[b], ref[other_b]], axis=0)

    panel_high, panel_low = ordered(block_high), ordered(block_low)

    def coupled_z(d):
        return copy(coupled.at[lax.rem(a + d, A)], z_coupled.at[d - 1], zc_s.at[d - 1], zc_r.at[d - 1], z_peer(d))

    for d in list(range(1, A)) + [0]:
        a_ = lax.rem(a + d, A)
        value = product(coup_high[a_], coup_low[a_], panel_high, panel_low).reshape(2, 2, qr, half)
        for g in range(2):
            for v in range(2):
                coupled[a_, g, v] = value[g, v] + own[2 + g, x, v, b, a_]
        if d:
            coupled_z(d).start()
    inverse_y(1).wait()
    inverse_core(1).start()
    got_inverse(1)
    end_first.wait()
    result(0)
    total = coupled[a]
    for d in range(1, A):
        coupled_z(d).wait()
        total = total + z_coupled[d - 1]
    gathered[1, a] = (side[1].reshape(block, half) - total.reshape(block, half)).reshape(2, 2 * qr, half)
    shard = gathered.at[1, a]
    last = [copy(shard, shard, g1_s.at[d - 1], g1_r.at[d - 1], z_peer(d)) for d in range(1, A)]
    start(last)
    second_panel = times_inverse(1, a)
    for d in range(1, A):
        last[d - 1].wait()
        second_panel = second_panel + times_inverse(1, lax.rem(a + A - d, A))
    end_second = finalize(1, second_panel)
    end_second.start()
    end_second.wait()
    result(1)


def body(R, C, panel_rows, solved, right_side, coupling, inverses):
    B = 2
    A, X = R // B, C // 2
    K = panel_rows.shape[2]
    tr, cw = right_side.shape[1:]
    qr, half, block, rows = B * tr // 4, cw // 2, B * tr, R * tr
    vmem, dma = pltpu.VMEM, pltpu.SemaphoreType.DMA
    steps = [(), (2,), (2,), (), (), (4, X), (4, X - 1), (4,), (4,), (4, X - 1), (2, A - 1), (2, A - 1), (A - 1,), (A - 1,), (2,)]
    sems = []
    for shape in steps:
        sems += [dma(shape) if shape else dma, dma(shape) if shape else dma]
    return pl.pallas_call(
        functools.partial(kernel, (A, B, X, K, tr, qr, cw)),
        out_shape=jax.ShapeDtypeStruct((2, tr, cw), F32),
        in_specs=[pl.BlockSpec(memory_space=pltpu.VMEM)] * 5,
        out_specs=pl.BlockSpec(memory_space=pltpu.VMEM),
        scratch_shapes=[
            vmem((4, 2, A * qr, 3 * K), BF16),
            vmem((C, 3 * K, cw), BF16),
            vmem((4, X, 2, B, A, qr, half), F32),
            vmem((4, X, 2, B, A, qr, half), F32),
            vmem((4, X, 2, B, A, qr, half), F32),
            vmem((4, X - 1, B, A, qr, half), F32),
            vmem((4, X, A, qr, half), F32),
            vmem((4, A, qr, half), F32),
            vmem((4, X - 1, A, qr, half), F32),
            vmem((2, A - 1, 2, qr, half), F32),
            vmem((B, 2, tr, half), F32),
            vmem((2, B, tr, half), F32),
            vmem((2, 2, tr // 2, rows), F32),
            vmem((2, A, B, tr, block), BF16),
            vmem((2, A, B, tr, block), BF16),
            vmem((2, rows // 2, tr), F32),
            vmem((A, block, B * tr), BF16),
            vmem((A, block, B * tr), BF16),
            vmem((2, A, 2, 2 * qr, half), F32),
            vmem((A, 2, 2, qr, half), F32),
            vmem((A - 1, 2, 2, qr, half), F32),
            vmem((B, tr, half), BF16),
            vmem((B, tr, half), BF16),
            vmem((2, B, tr, half), F32),
            vmem((2, tr, half), F32),
        ] + sems,
        compiler_params=pltpu.CompilerParams(
            collective_id=0, has_side_effects=True, vmem_limit_bytes=58 << 20
        ),
    )(
        panel_rows.reshape(2, A, 2, 2, qr, K),
        solved,
        right_side,
        coupling.reshape(2, rows // 2, tr),
        inverses.reshape(2, 2, tr // 2, rows),
    )


def solution(mesh):
    return jax.shard_map(
        functools.partial(body, mesh.shape["prow"], mesh.shape["pcol"]),
        mesh=mesh,
        in_specs=(
            P(None, None, ("prow", "pcol")),
            P(("prow", "pcol"), None),
            P(None, "prow", "pcol"),
            P(None, "prow"),
            P(None, "prow", None),
        ),
        out_specs=P(None, "prow", "pcol"),
        check_vma=False,
    )
```

time: 334 us -> 88 us (0.26)
  waiting for transfers between devices: 285 us -> 0 us
  Pallas kernels: 0 us -> 84.8 us
  matrix products: 26 us -> 0 us
  between operations: 13.2 us -> 0.01 us
    reduce_scatter x3 -> x0, waiting for transfers between devices: 205 us -> none  [the longest x1 72.8 us: combine_old(): lax.psum_scatter(partial_value, 'pcol', scatter_dimension=2, tiled=True)]
    pallas_call x0 -> x1, Pallas kernels: none -> 84.8 us  [body(): pl.pallas_call(functools.partial(kernel, (A, B, X, K, tr, qr, cw)), out_s...]
    all_gather x2 -> x0, waiting for transfers between devices: 79.4 us -> none  [apply_inverse(): lax.all_gather(residue, 'prow', axis=0, tiled=True)]
    dot_general x4 -> x0, matrix products: 26 us -> none  [the longest x1 16.7 us: body(): jnp.dot(flat_rows, solved, precision=highest, preferred_element_type=jnp....]
  transfers between devices with their start and end apart: 5 -> 0, of which waited for: 5 -> 0; matrix products, arithmetic and copies ran while one was open for 0% -> 0% of each run, Pallas kernels for 0% -> 0%
where the time goes in v2:
time: 88 us; the launch traced here: 86.5 us
  Pallas kernels  84.8 us (96%)
  local copies, waits for them, and re-layouts  1.67 us (2%)
    pallas_call x1, Pallas kernels, body(): pl.pallas_call(functools.partial(kernel, (A, B, X, K, tr, qr, cw)), out_s...  84.8 us

profile of v2, /device:TPU:24, one launch (start us, length us, event | category | flops | bytes accessed | tf_op | source)
XLA Modules:
  0.0 86.5 jit_solution(11857147204447715805)
XLA Ops:
  0.0 84.8 %shard_map.55 = f32[2,128,256]{2,1,0:T(8,128)} custom-call(f32[2,4,2,2,64,384]{5,4,3,2,1,0:T(8,128)} %bitcast.3, f32[384,1024]{1,0:T(8,128)} %solved.1, f32[2,128,256]{2,1,0:T(8,128)} %right_side.1, f32[2,512,128]{2,1,0:T(8,128)} %bitcast.5, f32[2,2,64,1024]{3,2,1,0:T(8,128)} %bitcast.4), custom_call_target="tpu_custom_call" | custom-call | tf_op jit(solution)/shard_map/pallas_call | solution.py:311
  84.9 1.7 %copy.7 = f32[2,128,256]{2,1,0:T(8,128)} copy(f32[2,128,256]{2,1,0:T(8,128)} %shard_map.55) | data formatting | bytes 524288

commit v3 on v2

--- a/solution.py
+++ b/solution.py
@@ -24,17 +24,19 @@
 
 
 def kernel(
-    sizes, panel, solved, right_side, coupling, inverses, out,
+    sizes, panel_hbm, solved_hbm, right_side, coupling_hbm, inverses_hbm, out,
+    panel, solved, coupling, inverses, in_sem,
     left, right, sent, received, own, x_u, y_v, y_u, x_v, z_last,
-    side_cut, side, inv_got, inv_high, inv_low, coup_got, coup_high, coup_low,
+    inv_got, inv_high, inv_low, coup_got, coup_high, coup_low,
     gathered, coupled, z_coupled, block_high, block_low, mine, theirs,
-    side_s, side_r, iy_s, iy_r, ic_s, ic_r, cy_s, cy_r, cc_s, cc_r,
+    iy_s, iy_r, ix_s, ix_r, ic_s, ic_r, cy_s, cy_r, cx_s, cx_r, cc_s, cc_r,
     core_s, core_r, xu_s, xu_r, yv_s, yv_r, yu_s, yu_r, xv_s, xv_r,
     zl_s, zl_r, g0_s, g0_r, zc_s, zc_r, g1_s, g1_r, end_s, end_r,
 ):
     A, B, X, K, tr, qr, cw = sizes
     half = cw // 2
     block = B * tr
+    width = A * block // (2 * X)
     row, col = lax.axis_index("prow"), lax.axis_index("pcol")
     a, b = row // B, row % B
     x, c = col // 2, col % 2
@@ -51,6 +53,16 @@
 
     def z_peer(d):
         return at(lax.rem(a + d, A), b, x, c)
+
+    def load(index, src, dst):
+        return pltpu.make_async_copy(src, dst, in_sem.at[index])
+
+    load_solved = load(0, solved_hbm, solved)
+    load_panel = [load(1 + t, panel_hbm.at[t // 2, :, t % 2], panel.at[t]) for t in range(4)]
+    load_inverses = load(5, inverses_hbm, inverses)
+    load_coupling = load(6, coupling_hbm, coupling)
+    for each in [load_solved] + load_panel + [load_inverses, load_coupling]:
+        each.start()
 
     peers = [core_peer, y_peer]
     peers += [x_peer(d) for d in range(1, X)] + [z_peer(d) for d in range(1, A)]
@@ -64,10 +76,6 @@
             device_id=peer, device_id_type=MESH,
         )
 
-    for b_ in range(B):
-        side_cut[b_] = right_side[:, :, b_ * half:(b_ + 1) * half]
-    side[:, b] = side_cut[b]
-
     def split_right(q):
         high, low = split(solved[:, q * cw:(q + 1) * cw])
         right[q, 0:K] = high
@@ -76,25 +84,29 @@
 
     def split_left(t):
         for v in range(2):
-            high, low = split(panel[t // 2, :, t % 2, v].reshape(A * qr, K))
+            high, low = split(panel[t, :, v].reshape(A * qr, K))
             left[t, v, :, 0:K] = high
             left[t, v, :, K:2 * K] = high
             left[t, v, :, 2 * K:] = low
 
-    pl.semaphore_wait(barrier, len(peers))
+    def columns(p):
+        return inverses.at[p, :, pl.ds(pl.multiple_of(col * width, width), width)]
 
     def inverse_y(p):
-        return copy(inverses.at[p, c], inv_got.at[p, c], iy_s.at[p], iy_r.at[p], y_peer)
+        return copy(columns(p), inv_got.at[p, c, x], iy_s.at[p], iy_r.at[p], y_peer)
+
+    def inverse_x(p, d):
+        return copy(inv_got.at[p, c, x], inv_got.at[p, c, x], ix_s.at[p, d - 1], ix_r.at[p, d - 1], x_peer(d))
 
     def inverse_core(p):
         return copy(inv_got.at[p, c], inv_got.at[p, c], ic_s.at[p], ic_r.at[p], core_peer)
 
-    coupling_y = copy(coupling.at[c], coup_got.at[c], cy_s, cy_r, y_peer)
+    def coupling_x(d):
+        return copy(coup_got.at[c, x], coup_got.at[c, x], cx_s.at[d - 1], cx_r.at[d - 1], x_peer(d))
+
+    coupling_y = copy(coupling.at[x, c], coup_got.at[c, x], cy_s, cy_r, y_peer)
     coupling_core = copy(coup_got.at[c], coup_got.at[c], cc_s, cc_r, core_peer)
-    side_y = copy(side_cut.at[other_b], side.at[:, b], side_s, side_r, y_peer)
-    inverse_y(0).start()
-    side_y.start()
-
+    load_solved.wait()
     for q in range(2 * X):
         split_right(q)
 
@@ -106,7 +118,10 @@
         return copy(sent.at[t, x_], received.at[t, x_], core_s.at[t, x_], core_r.at[t, x_], core_peer)
 
     def compute(t):
+        load_panel[t].wait()
         split_left(t)
+        if t == 0:
+            pl.semaphore_wait(barrier, len(peers))
 
         @pl.loop(0, X)
         def _(x_):
@@ -121,6 +136,12 @@
             core(t, x_).wait()
             for b_ in range(B):
                 own[t, x_, :, b_] = value[..., b_ * half:(b_ + 1) * half] + received[t, x_, :, b_]
+
+        for v in range(2):
+            for b_ in range(B):
+                ours = right_side[t // 2, v * qr:(v + 1) * qr, b_ * half:(b_ + 1) * half]
+                ours = jnp.where(b == t % 2, ours, jnp.zeros_like(ours))
+                own[t, x, v, b_, a] = own[t, x, v, b_, a] - ours
 
     def first_u(t):
         return [copy(own.at[t, lax.rem(x + d, X), 0], x_u.at[t, d - 1], xu_s.at[t, d - 1], xu_r.at[t, d - 1], x_peer(d)) for d in range(1, X)]
@@ -171,9 +192,9 @@
     def along_z(t):
         return [copy(own.at[t, x, :, b, lax.rem(a + d, A)], z_last.at[t, d - 1], zl_s.at[t, d - 1], zl_r.at[t, d - 1], z_peer(d)) for d in range(1, A)]
 
-    def gather_first(g):
+    def gather_first(g, d):
         shard = gathered.at[0, a, g]
-        return [copy(shard, shard, g0_s.at[g, d - 1], g0_r.at[g, d - 1], z_peer(d)) for d in range(1, A)]
+        return copy(shard, shard, g0_s.at[g, d - 1], g0_r.at[g, d - 1], z_peer(d))
 
     def rest(g):
         wait(along_z(g))
@@ -181,9 +202,9 @@
             total = own[g, x, v, b, a]
             for d in range(1, A):
                 total = total + z_last[g, d - 1, v]
-            at_row = (g * 2 + v) * qr
-            gathered[0, a, g, v * qr:(v + 1) * qr] = side[0, at_row // tr, at_row % tr:at_row % tr + qr] - total
-        start(gather_first(g))
+            gathered[0, a, g, v * qr:(v + 1) * qr] = -total
+        for d in range(1, A):
+            gather_first(g, d).start()
 
     def hold_inverse(p, b_, value):
         for a_ in range(A):
@@ -193,7 +214,11 @@
 
     def got_inverse(p):
         inverse_core(p).wait()
-        hold_inverse(p, other_b, inv_got[p].reshape(tr, A * block))
+        for a_ in range(A):
+            piece, offset = a_ * block // width, a_ * block % width
+            high, low = split(inv_got[p, piece % 2, piece // 2, :, offset:offset + block])
+            inv_high[p, a_, other_b] = high
+            inv_low[p, a_, other_b] = low
 
     def times_inverse(p, a_):
         high, low = split(gathered[p, a_].reshape(block, half))
@@ -205,42 +230,54 @@
     compute(1)
     turn(0)
     start_first(1)
-    inverse_y(0).wait()
-    inverse_core(0).start()
     compute(2)
     finish(0)
     start(along_z(0))
     turn(1)
     start_first(2)
+    load_inverses.wait()
+    load_coupling.wait()
+    inverse_y(0).start()
     coupling_y.start()
     compute(3)
     finish(1)
     start(along_z(1))
+    rest(0)
     turn(2)
     start_first(3)
-    side_y.wait()
-    rest(0)
-    hold_inverse(0, b, inverses[0].reshape(tr, A * block))
-    got_inverse(0)
+    hold_inverse(0, b, inverses[0])
+    inverse_y(0).wait()
+    for d in range(1, X):
+        inverse_x(0, d).start()
+    coupling_y.wait()
+    for d in range(1, X):
+        coupling_x(d).start()
     rest(1)
     high, low = split(coupling[...].reshape(A, block, tr))
     coup_high[:, :, 0:tr] = high
     coup_low[:, :, 0:tr] = low
-    coupling_y.wait()
-    coupling_core.start()
     finish(2)
     turn(3)
     inverse_y(1).start()
+    for d in range(1, X):
+        inverse_x(0, d).wait()
+    inverse_core(0).start()
+    for d in range(1, X):
+        coupling_x(d).wait()
+    coupling_core.start()
+    hold_inverse(1, b, inverses[1])
+    got_inverse(0)
     coupling_core.wait()
-    high, low = split(coup_got[...].reshape(A, block, tr))
-    coup_high[:, :, tr:] = high
-    coup_low[:, :, tr:] = low
-    hold_inverse(1, b, inverses[1].reshape(tr, A * block))
+    many = width // block
+    for q in range(2 * X):
+        high, low = split(coup_got[q % 2, q // 2].reshape(many, block, tr))
+        coup_high[q * many:(q + 1) * many, :, tr:] = high
+        coup_low[q * many:(q + 1) * many, :, tr:] = low
 
     first_panel = times_inverse(0, a)
     for d in range(1, A):
         for g in range(2):
-            gather_first(g)[d - 1].wait()
+            gather_first(g, d).wait()
         first_panel = first_panel + times_inverse(0, lax.rem(a + A - d, A))
 
     def finalize(p, value):
@@ -254,6 +291,9 @@
 
     end_first = finalize(0, first_panel)
     end_first.start()
+    inverse_y(1).wait()
+    for d in range(1, X):
+        inverse_x(1, d).start()
     for each, ref in zip(split(first_panel.reshape(B, tr, half)), (block_high, block_low)):
         ref[...] = each
     finish(3)
@@ -274,7 +314,8 @@
                 coupled[a_, g, v] = value[g, v] + own[2 + g, x, v, b, a_]
         if d:
             coupled_z(d).start()
-    inverse_y(1).wait()
+    for d in range(1, X):
+        inverse_x(1, d).wait()
     inverse_core(1).start()
     got_inverse(1)
     end_first.wait()
@@ -283,14 +324,37 @@
     for d in range(1, A):
         coupled_z(d).wait()
         total = total + z_coupled[d - 1]
-    gathered[1, a] = (side[1].reshape(block, half) - total.reshape(block, half)).reshape(2, 2 * qr, half)
-    shard = gathered.at[1, a]
-    last = [copy(shard, shard, g1_s.at[d - 1], g1_r.at[d - 1], z_peer(d)) for d in range(1, A)]
-    start(last)
-    second_panel = times_inverse(1, a)
-    for d in range(1, A):
-        last[d - 1].wait()
-        second_panel = second_panel + times_inverse(1, lax.rem(a + A - d, A))
+    gathered[1, a] = -total.reshape(2, 2 * qr, half)
+
+    def hop(held, step):
+        block_ref = gathered.at[1, lax.rem(a + A - held, A)]
+        return copy(block_ref, block_ref, g1_s.at[step], g1_r.at[step], z_peer(1))
+
+    @pl.when(a < A - 1)
+    def _():
+        hop(0, 0).start()
+
+    mine[1] = times_inverse(1, a).reshape(B, tr, half)
+    for step in range(1, A):
+
+        @pl.when(a >= step)
+        def _():
+            hop(step, step - 1).wait_recv()
+            if step < A - 1:
+
+                @pl.when(a < A - 1)
+                def _():
+                    hop(step, step).start()
+
+            mine[1] = mine[1] + times_inverse(1, lax.rem(a + A - step, A)).reshape(B, tr, half)
+
+    for step in range(A - 1):
+
+        @pl.when((a < A - 1) & (a >= step))
+        def _():
+            hop(step, step).wait_send()
+
+    second_panel = mine[1]
     end_second = finalize(1, second_panel)
     end_second.start()
     end_second.wait()
@@ -304,16 +368,21 @@
     tr, cw = right_side.shape[1:]
     qr, half, block, rows = B * tr // 4, cw // 2, B * tr, R * tr
     vmem, dma = pltpu.VMEM, pltpu.SemaphoreType.DMA
-    steps = [(), (2,), (2,), (), (), (4, X), (4, X - 1), (4,), (4,), (4, X - 1), (2, A - 1), (2, A - 1), (A - 1,), (A - 1,), (2,)]
+    steps = [(2,), (2, X - 1), (2,), (), (X - 1,), (), (4, X), (4, X - 1), (4,), (4,), (4, X - 1), (2, A - 1), (2, A - 1), (A - 1,), (A - 1,), (2,)]
     sems = []
     for shape in steps:
         sems += [dma(shape) if shape else dma, dma(shape) if shape else dma]
     return pl.pallas_call(
         functools.partial(kernel, (A, B, X, K, tr, qr, cw)),
         out_shape=jax.ShapeDtypeStruct((2, tr, cw), F32),
-        in_specs=[pl.BlockSpec(memory_space=pltpu.VMEM)] * 5,
+        in_specs=[pl.BlockSpec(memory_space=pltpu.VMEM if i == 2 else pl.ANY) for i in range(5)],
         out_specs=pl.BlockSpec(memory_space=pltpu.VMEM),
         scratch_shapes=[
+            vmem((4, A, 2, qr, K), F32),
+            vmem((K, C * cw), F32),
+            vmem((X, 2, rows // C, tr), F32),
+            vmem((2, tr, rows), F32),
+            dma((7,)),
             vmem((4, 2, A * qr, 3 * K), BF16),
             vmem((C, 3 * K, cw), BF16),
             vmem((4, X, 2, B, A, qr, half), F32),
@@ -324,12 +393,10 @@
             vmem((4, A, qr, half), F32),
             vmem((4, X - 1, A, qr, half), F32),
             vmem((2, A - 1, 2, qr, half), F32),
-            vmem((B, 2, tr, half), F32),
-            vmem((2, B, tr, half), F32),
-            vmem((2, 2, tr // 2, rows), F32),
+            vmem((2, 2, X, tr, rows // C), F32),
             vmem((2, A, B, tr, block), BF16),
             vmem((2, A, B, tr, block), BF16),
-            vmem((2, rows // 2, tr), F32),
+            vmem((2, X, rows // C, tr), F32),
             vmem((A, block, B * tr), BF16),
             vmem((A, block, B * tr), BF16),
             vmem((2, A, 2, 2 * qr, half), F32),
@@ -347,8 +414,8 @@
         panel_rows.reshape(2, A, 2, 2, qr, K),
         solved,
         right_side,
-        coupling.reshape(2, rows // 2, tr),
-        inverses.reshape(2, 2, tr // 2, rows),
+        coupling.reshape(X, 2, rows // C, tr),
+        inverses,
     )
 
 

time: 88 us -> 84.4 us (0.959); the launches traced: 86.5 us -> 84.2 us
  Pallas kernels: 84.8 us -> 82.5 us
    pallas_call x1, Pallas kernels: 84.8 us -> 82.5 us  [body(): pl.pallas_call(functools.partial(kernel, (A, B, X, K, tr, qr, cw)), out_s...]
where the time goes in v3:
time: 84.4 us; the launch traced here: 84.2 us
  Pallas kernels  82.5 us (98%)
  local copies, waits for them, and re-layouts  1.67 us (2%)
    pallas_call x1, Pallas kernels, body(): pl.pallas_call(functools.partial(kernel, (A, B, X, K, tr, qr, cw)), out_s...  82.5 us

profile of v3, /device:TPU:24, one launch (start us, length us, event | category | flops | bytes accessed | tf_op | source)
XLA Modules:
  0.0 84.2 jit_solution(14933014679358312158)
XLA Ops:
  0.0 82.5 %shard_map.55 = f32[2,128,256]{2,1,0:T(8,128)} custom-call(f32[2,4,2,2,64,384]{5,4,3,2,1,0:T(8,128)} %bitcast.2, f32[384,1024]{1,0:T(8,128)} %solved_hbm.1, f32[2,128,256]{2,1,0:T(8,128)} %right_side.1, f32[2,2,256,128]{3,2,1,0:T(8,128)} %bitcast.3, f32[2,128,1024]{2,1,0:T(8,128)} %inverses_hbm.1), custom_call_target="tpu_custom_call" | custom-call | tf_op jit(solution)/shard_map/pallas_call | solution.py:375
  82.5 1.7 %copy.7 = f32[2,128,256]{2,1,0:T(8,128)} copy(f32[2,128,256]{2,1,0:T(8,128)} %shard_map.55) | data formatting | bytes 524288
